TPU v7x, 32 devices: a whole 2x2x4 slice. The times are simulated.
32 devices in a mesh: groups: 2 (over x), team: 2 (over core), blk: 8 (over z, y).
Axes of the slice: x: 2, y: 2, z: 4, core: 2. Of those that a mesh axis runs over, the one named last changes fastest.
Arguments:
- probe: bfloat16 [192, 32, 128], P(('groups', 'blk')), parts along dimension 0, may hold values from -6 to 6
- positions: float32 [192, 3, 128], P(('groups', 'blk')), parts along dimension 0, as said below
- conductivity: float32 [192, 128], P(('groups', 'blk')), parts along dimension 0, may hold values from 0.5 to 2
- fluid_exchange: float32 [192, 128], P(('groups', 'blk')), parts along dimension 0, may hold values from 0.5 to 8
- row_blocks: int32 [192], P(('groups', 'blk')), parts along dimension 0, may hold values from 1 to 27, 864 in all
- column_blocks: int32 [192, 27], P(('groups', 'blk')), parts along dimension 0, may hold values from 0 to 95, as said below
Outputs:
- filtered: float32 [192, 32, 128], P(('groups', 'blk')), parts along dimension 0
There are 2 independent parts, one for each index of `groups`. A program takes and returns all parts, laid end to end along the dimension named above; each array names one. Nothing has to cross between parts.
Inputs may be any that keep to these rules, and one draw needn't show every extreme that they name: `row_blocks`: every row lists at least one block; the counts of one bed sum to 864. `column_blocks`: ids in slots at or beyond a row's count are ignored; ids may repeat within a row. Every id differs from its row I by at most 24 around the closed order of the 96 clusters (J = (I + d) mod 96, |d| <= 24), and both ends of that reach occur. `positions`: clusters close in index lie close in space.
All inputs are finite; a program needn't handle non-finite values.
Results may differ from a plain program's by a relative error of at most 0.0029.
Values may be sent and summed in bfloat16 or wider, within the bound.
A program may use at most 64 MiB of HBM per device.

v0:
```python
import functools
import math

import jax
import jax.numpy as jnp
from jax import lax
from jax.experimental import pallas as pl
from jax.experimental.pallas import tpu as pltpu
from jax.sharding import PartitionSpec as P

DEGREE = 8
WIDTH_SQ = 0.245
CENTER = 1.05
HALF_SPAN = 0.95
SCALE = math.sqrt(math.log2(math.e) / WIDTH_SQ)
MESH = pl.DeviceIdType.MESH
REACHES = (-2, -1, 1, 2)
CHUNK = 3


def kernel(
    teams, probe_in, pos_in, cond_in, fluid_in, counts_in, cols_in, out,
    probe, pos, cond, fluid, counts, cols, load_sem,
    geo, bcast, tiles, even, odd, cur, prev, inv, corr, ids, other,
    geo_send, geo_recv, win_send, win_recv, pair_send, pair_recv,
):
    loads = [
        pltpu.make_async_copy(source, place, load_sem.at[n])
        for n, (source, place) in enumerate(
            (
                (pos_in, pos), (cond_in, cond), (probe_in, probe),
                (cols_in, cols), (counts_in, counts), (fluid_in, fluid),
            )
        )
    ]
    for load in loads:
        load.start()
    rows, columns, particles = probe.shape
    half = columns // 2
    slots = cols.shape[1]
    clusters = teams * rows
    group = lax.axis_index("groups")
    member = lax.axis_index("team")
    team = lax.axis_index("blk")

    def at(reach):
        return (group, member, lax.rem(team + reach + teams, teams))

    partner = (group, 1 - member, team)
    barrier = pltpu.get_barrier_semaphore()
    for reach in REACHES:
        pl.semaphore_signal(barrier, inc=1, device_id=at(reach), device_id_type=MESH)
    pl.semaphore_signal(barrier, inc=1, device_id=partner, device_id_type=MESH)

    for load in loads[:3]:
        load.wait()
    for r in range(rows):
        geo[2, r, 0:3, :] = pos[r] * SCALE
        geo[2, r, 3:4, :] = 0.5 / cond[r : r + 1, :]
        mine = probe[r, pl.ds(pl.multiple_of(member * half, half), half), :]
        even[2 * rows + r] = mine
        cur[r] = mine.astype(jnp.float32)
        prev[r] = jnp.zeros((half, particles), jnp.float32)
    pl.semaphore_wait(barrier, len(REACHES) + 1)

    def geo_copy(n):
        reach = REACHES[n]
        return pltpu.make_async_remote_copy(
            src_ref=geo.at[2], dst_ref=geo.at[2 - reach],
            send_sem=geo_send.at[n], recv_sem=geo_recv.at[n],
            device_id=at(reach), device_id_type=MESH,
        )

    def win_copy(parity, n, first=0, size=None):
        reach = REACHES[n]
        window = (even, odd)[parity]
        size = rows if size is None else size
        return pltpu.make_async_remote_copy(
            src_ref=window.at[pl.ds(2 * rows + first, size)], dst_ref=window.at[pl.ds((2 - reach) * rows + first, size)],
            send_sem=win_send.at[parity, n], recv_sem=win_recv.at[parity, n],
            device_id=at(reach), device_id_type=MESH,
        )

    for n in range(4):
        geo_copy(n).start()
    def spread(place):
        def one(r, carry):
            for k in range(4):
                line = geo[place, r, k : k + 1, :]
                bcast[place * rows + r, k] = jnp.broadcast_to(line, (particles, particles)).T
            return carry
        lax.fori_loop(0, rows, one, 0, unroll=2)

    spread(2)
    for n in range(4):
        geo_copy(n).wait()
        spread(2 - REACHES[n])
    for n in range(4):
        win_copy(0, n).start()

    for load in loads[3:]:
        load.wait()
    base = (team - 2) * rows

    def build_row(r, carry):
        own = team * rows + r
        count = counts[r]
        xi = [jnp.broadcast_to(geo[2, r, k : k + 1, :], (8, particles)) for k in range(4)]

        def build_tile(s, state):
            total, selves = state
            col = cols[r, s]
            active = s < count
            place = col - base
            place = jnp.where(place < 0, place + clusters, place)
            place = jnp.where(place >= clusters, place - clusters, place)
            place = jnp.where(active, jnp.minimum(place, 5 * rows - 1), 0)
            ids[r, s] = place
            selves = selves + jnp.where(active & (col == own), 1.0, 0.0)
            bias = jnp.where(active, 0.0, -1e30)
            for j in range(0, particles, 16):
                parts = []
                for h in (j, j + 8):
                    dx = bcast[place, 0, h : h + 8, :] - xi[0]
                    dy = bcast[place, 1, h : h + 8, :] - xi[1]
                    dz = bcast[place, 2, h : h + 8, :] - xi[2]
                    power = bias - dx * dx - dy * dy - dz * dz
                    value = jnp.exp2(power) / (bcast[place, 3, h : h + 8, :] + xi[3])
                    total = total + value
                    parts.append(value)
                tiles[r, pl.ds(pl.multiple_of(s * particles + j, 16), 16), :] = jnp.concatenate(
                    parts, 0
                ).astype(jnp.bfloat16)
            return total, selves

        total, selves = lax.fori_loop(
            0, slots, build_tile, (jnp.zeros((8, particles), jnp.float32), jnp.float32(0.0)),
            unroll=3,
        )
        itself = 1.0 / (xi[3] + xi[3])
        degree = jnp.sum(total, axis=0, keepdims=True) - selves * itself[0:1]
        divisor = fluid[pl.ds(r, 1), :] + degree
        inv[r] = jnp.broadcast_to((2.0 / HALF_SPAN) / divisor, (half, particles))
        rounded = itself[0:1].astype(jnp.bfloat16).astype(jnp.float32)
        corr[r] = jnp.broadcast_to(selves * rounded, (half, particles))
        return carry

    lax.fori_loop(0, rows, build_row, 0)

    def step(k, now):
        later = 1 - now
        window, target = (even, odd)[now], (even, odd)[later]
        for n in range(4):
            win_copy(now, n).wait()
        gain = jnp.where(k == 0, 0.5, 1.0)

        def row(r):
            taken = jnp.concatenate(
                [window[ids[r, s]] for s in range(slots)],
                axis=1,
            )
            product = jnp.dot(taken, tiles[r], preferred_element_type=jnp.float32)
            mine = window[2 * rows + r].astype(jnp.float32)
            product = product - corr[r] * mine
            field = cur[r]
            change = (2.0 * (1.0 - CENTER) / HALF_SPAN) * field - product * inv[r]
            fresh = gain * change - prev[r]
            prev[r] = field
            cur[r] = fresh
            target[2 * rows + r] = fresh.astype(jnp.bfloat16)

        for first in range(0, rows, CHUNK):
            size = min(CHUNK, rows - first)
            for r in range(first, first + size):
                row(r)

            @pl.when(k < DEGREE - 1)
            def _():
                for n in range(4):
                    win_copy(later, n, first, size).start()

    def two_steps(i, carry):
        step(2 * i, 0)
        step(2 * i + 1, 1)
        return carry

    lax.fori_loop(0, DEGREE // 2, two_steps, 0)

    swap = pltpu.make_async_remote_copy(
        src_ref=cur, dst_ref=other, send_sem=pair_send, recv_sem=pair_recv,
        device_id=partner, device_id_type=MESH,
    )
    swap.start()
    out[:, pl.ds(pl.multiple_of(member * half, half), half), :] = cur[...]
    swap.wait()
    out[:, pl.ds(pl.multiple_of((1 - member) * half, half), half), :] = other[...]


def local(teams, probe, positions, conductivity, fluid_exchange, row_blocks, column_blocks):
    rows, columns, particles = probe.shape
    slots = column_blocks.shape[1]
    half = columns // 2
    vmem = pl.BlockSpec(memory_space=pltpu.VMEM)
    anywhere = pl.BlockSpec(memory_space=pl.ANY)
    f32 = jnp.float32
    return pl.pallas_call(
        functools.partial(kernel, teams),
        out_shape=jax.ShapeDtypeStruct((rows, columns, particles), f32),
        in_specs=[anywhere] * 6,
        out_specs=vmem,
        scratch_shapes=[
            pltpu.VMEM(probe.shape, probe.dtype),
            pltpu.VMEM(positions.shape, f32),
            pltpu.VMEM(conductivity.shape, f32),
            pltpu.VMEM(fluid_exchange.shape, f32),
            pltpu.SMEM(row_blocks.shape, jnp.int32),
            pltpu.SMEM(column_blocks.shape, jnp.int32),
            pltpu.SemaphoreType.DMA((6,)),
            pltpu.VMEM((5, rows, 4, particles), f32),
            pltpu.VMEM((5 * rows, 4, particles, particles), f32),
            pltpu.VMEM((rows, slots * particles, particles), jnp.bfloat16),
            pltpu.VMEM((5 * rows, half, particles), jnp.bfloat16),
            pltpu.VMEM((5 * rows, half, particles), jnp.bfloat16),
            pltpu.VMEM((rows, half, particles), f32),
            pltpu.VMEM((rows, half, particles), f32),
            pltpu.VMEM((rows, half, particles), f32),
            pltpu.VMEM((rows, half, particles), f32),
            pltpu.SMEM((rows, slots), jnp.int32),
            pltpu.VMEM((rows, half, particles), f32),
            pltpu.SemaphoreType.DMA((4,)),
            pltpu.SemaphoreType.DMA((4,)),
            pltpu.SemaphoreType.DMA((2, 4)),
            pltpu.SemaphoreType.DMA((2, 4)),
            pltpu.SemaphoreType.DMA,
            pltpu.SemaphoreType.DMA,
        ],
        compiler_params=pltpu.CompilerParams(
            collective_id=0, has_side_effects=True, vmem_limit_bytes=60 * 1024 * 1024
        ),
    )(probe, positions, conductivity, fluid_exchange, row_blocks, column_blocks)


def solution(mesh):
    return jax.shard_map(
        functools.partial(local, mesh.shape["blk"]),
        mesh=mesh,
        in_specs=(
            P(("groups", "blk"), None, None),
            P(("groups", "blk"), None, None),
            P(("groups", "blk"), None),
            P(("groups", "blk"), None),
            P(("groups", "blk")),
            P(("groups", "blk"), None),
        ),
        out_specs=P(("groups", "blk"), None, None),
        check_vma=False,
    )
```

profile of v0, /device:TPU:0, one launch (start us, length us, event | category | flops | bytes accessed | tf_op | source)
XLA Modules:
  0.0 77.7 jit_solution(16956839524899780002)
XLA Ops:
  0.0 76.1 %shard_map.64 = f32[12,32,128]{2,1,0:T(8,128)} custom-call(bf16[12,32,128]{2,1,0:T(8,128)(2,1)} %probe_in.1, f32[12,3,128]{2,1,0:T(4,128)} %pos_in.1, f32[12,128]{1,0:T(8,128)} %cond_in.1, f32[12,128]{1,0:T(8,128)} %fluid_in.1, s32[12]{0:T(128)} %counts_in.1, s32[12,27]{1,0:T(8,128)} %cols_in.1), custom_call_target="tpu_custom_call" | custom-call | tf_op jit(solution)/shard_map/pallas_call | solution.py:206
  76.1 1.6 %copy.8 = f32[12,32,128]{2,1,0:T(8,128)} copy(f32[12,32,128]{2,1,0:T(8,128)} %shard_map.64) | data formatting | bytes 393216
where the time goes:
time: 77.8 us; the launch traced here: 77.7 us
  Pallas kernels  76.1 us (98%)
  local copies, waits for them, and re-layouts  1.62 us (2%)
    pallas_call x1, Pallas kernels, local(): pl.pallas_call(functools.partial(kernel, teams), out_shape=jax.ShapeDtype...  76.1 us
    unnamed x1, local copies, waits for them, and re-layouts  1.62 us

commit v1 on v0

--- a/solution.py
+++ b/solution.py
@@ -16,6 +16,9 @@
 MESH = pl.DeviceIdType.MESH
 REACHES = (-2, -1, 1, 2)
 CHUNK = 3
+MEAN_BLOCKS = 9
+APPROX = True
+UNROLL = 54
 
 
 def kernel(
@@ -240,9 +243,378 @@
     )(probe, positions, conductivity, fluid_exchange, row_blocks, column_blocks)
 
 
+def bed_kernel(
+    teams, total, probe_in, pos_in, cond_in, fluid_in, counts_in, cols_in, out,
+    probe, pos, cond, load_sem,
+    geo, ints, cnts, counts, cols, smem_sem, fluid, stage, landed,
+    bcast, tiles, ends, begins, ids, keep, selfs, more, last,
+    sums, parts, low, high, cur, prev, inv, corr, mine_sum, their_sum, mine_deg, their_deg, arrived,
+    gather_send, gather_recv, pair_send, pair_recv,
+):
+    rows, columns, particles = probe.shape
+    slots = cols.shape[1]
+    clusters = teams * rows
+    width = columns // teams
+    pairs = clusters // 2
+    units = tiles.shape[0]
+    span = 2 * units
+    group = lax.axis_index("groups")
+    member = lax.axis_index("team")
+    team = lax.axis_index("blk")
+    f32, bf16 = jnp.float32, jnp.bfloat16
+
+    def at(ahead):
+        return (group, member, lax.rem(team + ahead, teams))
+
+    partner = (group, 1 - member, team)
+    barrier = pltpu.get_barrier_semaphore()
+    for ahead in range(1, teams):
+        pl.semaphore_signal(barrier, inc=1, device_id=at(ahead), device_id_type=MESH)
+    pl.semaphore_signal(barrier, inc=1, device_id=partner, device_id_type=MESH)
+
+    loads = [
+        pltpu.make_async_copy(source, place, load_sem.at[n])
+        for n, (source, place) in enumerate(
+            (
+                (pos_in, pos), (cond_in, cond), (probe_in, probe),
+                (cols_in, ints.at[team]), (counts_in, cnts.at[team]), (fluid_in, fluid.at[team]),
+            )
+        )
+    ]
+    for load in loads:
+        load.start()
+    for load in loads[:2]:
+        load.wait()
+    for r in range(rows):
+        geo[team, r, 0:3, :] = pos[r] * SCALE
+        geo[team, r, 3:4, :] = 0.5 / cond[r : r + 1, :]
+    pl.semaphore_wait(barrier, teams)
+
+    def gather(kind, ahead):
+        source, place = (
+            (counts_in, cnts.at[team]), (cols_in, ints.at[team]), (geo.at[team], geo.at[team]),
+            (stage.at[lax.rem(team + ahead, teams)], landed.at[team]), (fluid_in, fluid.at[team]),
+        )[kind]
+        return pltpu.make_async_remote_copy(
+            src_ref=source, dst_ref=place,
+            send_sem=gather_send.at[kind, ahead], recv_sem=gather_recv.at[kind, ahead],
+            device_id=at(ahead), device_id_type=MESH,
+        )
+
+    others = range(1, teams)
+    for load in loads[3:5]:
+        load.wait()
+    for ahead in others:
+        gather(2, ahead).start()
+    for ahead in others:
+        gather(0, ahead).start()
+        gather(1, ahead).start()
+
+    def spread(place):
+        def one(r, carry):
+            for k in range(4):
+                line = geo[place, r, k : k + 1, :]
+                bcast[place * rows + r, k] = jnp.broadcast_to(line, (particles, particles)).T
+            return carry
+        lax.fori_loop(0, rows, one, 0, unroll=4)
+
+    spread(team)
+    loads[2].wait()
+    loads[5].wait()
+    for q in range(rows // 4):
+        wide = [probe[4 * q + a].astype(f32) for a in range(4)]
+        for t in range(teams):
+            stage[t, q] = jnp.concatenate([w[t * width : (t + 1) * width] for w in wide], 0).astype(bf16)
+    landed[team] = stage[team]
+    for ahead in others:
+        gather(0, ahead).wait()
+        gather(1, ahead).wait()
+    moves = [
+        pltpu.make_async_copy(cnts, counts, smem_sem.at[teams]),
+    ] + [
+        pltpu.make_async_copy(ints.at[t], cols.at[pl.ds(t * rows, rows)], smem_sem.at[t]) for t in range(teams)
+    ]
+    for move in moves:
+        move.start()
+    for ahead in others:
+        gather(2, ahead).wait()
+        spread(lax.rem(team + teams - ahead, teams))
+    for ahead in others:
+        gather(3, ahead).start()
+        gather(4, ahead).start()
+    for move in moves:
+        move.wait()
+
+    first = member * span
+    final = first + span
+
+    def lay(t, state):
+        at_end, zero, one = state
+        for j in range(rows):
+            r = t * rows + j
+            begins[r] = at_end
+            at_end = at_end + counts[t, 0, j]
+            ends[r] = at_end
+            zero = zero + jnp.where(at_end <= first, 1, 0)
+            one = one + jnp.where(at_end <= first + units, 1, 0)
+        return at_end, zero, one
+
+    _, zero, one = lax.fori_loop(0, teams, lay, (jnp.int32(0), jnp.int32(0), jnp.int32(0)))
+    zero, one = jnp.minimum(zero, clusters - 1), jnp.minimum(one, clusters - 1)
+
+    def build_tile(u, lane, r, selves, running):
+        place = first + lane * units + u
+        index = lane * units + u
+        r = jnp.minimum(r + jnp.where(place >= ends[r], 1, 0), clusters - 1)
+        begin = begins[r]
+        col = cols[r, jnp.minimum(place - begin, slots - 1)]
+        fresh = jnp.logical_or(place == begin, u == 0)
+        going = jnp.where(fresh, 0.0, 1.0)
+        ids[index] = col
+        keep[index] = going
+        selves = jnp.where(fresh, 0.0, selves) + jnp.where(col == r, 1.0, 0.0)
+        selfs[index] = selves
+        t = lax.div(r, rows)
+        xi = [jnp.broadcast_to(geo[t, r - t * rows, k : k + 1, :], (8, particles)) for k in range(4)]
+        tally = jnp.zeros((8, particles), f32)
+        for j in range(0, particles, 16):
+            values = []
+            for h in (j, j + 8):
+                dx = bcast[col, 0, h : h + 8, :] - xi[0]
+                dy = bcast[col, 1, h : h + 8, :] - xi[1]
+                dz = bcast[col, 2, h : h + 8, :] - xi[2]
+                power = dx * dx + dy * dy + dz * dz
+                value = pltpu.reciprocal((bcast[col, 3, h : h + 8, :] + xi[3]) * jnp.exp2(power), approx=APPROX)
+                tally = tally + value
+                values.append(value)
+            tiles[u, lane * particles + j : lane * particles + j + 16, :] = jnp.concatenate(values, 0).astype(bf16)
+        running = running * going + tally
+        sums[index] = running
+        return r, selves, running
+
+    def build(u, state):
+        return build_tile(u, 0, *state[:3]) + build_tile(u, 1, *state[3:])
+
+    blank = jnp.zeros((8, particles), f32)
+    state = lax.fori_loop(
+        0, units, build, (zero, jnp.float32(0.0), blank, one, jnp.float32(0.0), blank), unroll=2
+    )
+
+    sums[span] = blank
+    parts[span] = blank
+    edge_row = state[0]
+    edge = ends[edge_row]
+    for u in range(slots - 1):
+        flag = jnp.where(first + units + u < edge, 1.0, 0.0)
+        more[u] = flag
+        selfs[units + u] = selfs[units + u] + flag * selfs[units - 1]
+        sums[units + u] = sums[units + u] + flag * sums[units - 1]
+    half = lax.broadcasted_iota(jnp.int32, (8, particles), 0) < width
+
+    def both(even, odd):
+        return jnp.where(half, jnp.broadcast_to(even, (8, particles)), jnp.broadcast_to(odd, (8, particles)))
+
+    def settle(t, carry):
+        for j in range(0, rows, 2):
+            r = t * rows + j
+            p = t * (rows // 2) + j // 2
+            lines = []
+            for h in (0, 1):
+                end = jnp.minimum(ends[r + h], final) - 1
+                have = end >= jnp.maximum(begins[r + h], first)
+                spot = jnp.where(have, end - first, span)
+                last[r + h] = spot
+                own = jnp.where(have, selfs[jnp.where(have, end - first, 0)], 0.0)
+                twice = geo[t, j + h, 3:4, :] + geo[t, j + h, 3:4, :]
+                itself = pltpu.reciprocal(twice, approx=APPROX)
+                degree = jnp.sum(sums[spot], axis=0, keepdims=True) - own * itself
+                lines.append((degree, own * itself.astype(bf16).astype(f32)))
+            mine_deg[p] = both(lines[0][0], lines[1][0])
+            corr[p] = both(lines[0][1], lines[1][1])
+        return carry
+
+    lax.fori_loop(0, teams, settle, 0)
+
+    def swap(source, place, n):
+        return pltpu.make_async_remote_copy(
+            src_ref=source, dst_ref=place, send_sem=pair_send.at[n], recv_sem=pair_recv.at[n],
+            device_id=partner, device_id_type=MESH,
+        )
+
+    degrees = swap(mine_deg, their_deg, 2)
+    degrees.start()
+
+    nothing = jnp.zeros((8, particles), f32)
+
+    def publish(p, fresh):
+        turned = pltpu.roll(fresh, width, 0)
+        for h, line in ((0, jnp.where(half, fresh, turned)), (1, jnp.where(half, turned, fresh))):
+            low[2 * p + h] = jnp.concatenate([line, nothing], 0).astype(bf16)
+            high[2 * p + h] = jnp.concatenate([nothing, line], 0).astype(bf16)
+
+    for ahead in others:
+        gather(3, ahead).wait()
+        gather(4, ahead).wait()
+
+    def begin_fields(t, carry):
+        for q in range(rows // 4):
+            block = landed[t, q].astype(f32)
+            for h in (0, 1):
+                p = t * (rows // 2) + 2 * q + h
+                cur[p] = block[8 * h : 8 * h + 8]
+                prev[p] = nothing
+                publish(p, block[8 * h : 8 * h + 8])
+        return carry
+
+    lax.fori_loop(0, teams, begin_fields, 0)
+
+    degrees.wait()
+
+    def divide(t, carry):
+        for j in range(0, rows, 2):
+            p = t * (rows // 2) + j // 2
+            exchange = both(fluid[t, j : j + 1, :], fluid[t, j + 1 : j + 2, :])
+            inv[p] = (2.0 / HALF_SPAN) / (exchange + (mine_deg[p] + their_deg[p]))
+        return carry
+
+    lax.fori_loop(0, teams, divide, 0)
+
+    def step(k, carry):
+        slot = lax.rem(k, 2)
+
+        def unit(u, state):
+            taken = jnp.concatenate([low[ids[u]], high[ids[units + u]]], axis=1)
+            product = jnp.dot(taken, tiles[u], preferred_element_type=f32)
+            zero = state[0] * keep[u] + product[0:8]
+            one = state[1] * keep[units + u] + product[8:16]
+            parts[u] = zero
+            parts[units + u] = one
+            return zero, one
+
+        lax.fori_loop(0, units, unit, (blank, blank), unroll=UNROLL)
+        for u in range(slots - 1):
+            parts[units + u] = parts[units + u] + more[u] * parts[units - 1]
+
+        def pack(p, carry):
+            own = cur[p].astype(bf16).astype(f32)
+            product = jnp.where(half, parts[last[2 * p]], parts[last[2 * p + 1]])
+            mine_sum[slot, p] = product - corr[p] * own
+            return carry
+
+        lax.fori_loop(0, pairs, pack, 0, unroll=8)
+        exchange = swap(mine_sum.at[slot], their_sum.at[slot], slot)
+        exchange.start()
+        exchange.wait()
+        gain = jnp.where(k == 0, 0.5, 1.0)
+
+        def update(p, carry):
+            field = cur[p]
+            product = mine_sum[slot, p] + their_sum[slot, p]
+            change = (2.0 * (1.0 - CENTER) / HALF_SPAN) * field - product * inv[p]
+            fresh = gain * change - prev[p]
+            prev[p] = field
+            cur[p] = fresh
+            publish(p, fresh)
+            return carry
+
+        lax.fori_loop(0, pairs, update, 0, unroll=8)
+        return carry
+
+    lax.fori_loop(0, DEGREE, step, 0)
+
+    few = rows // 2
+
+    def deliver(ahead):
+        goal = lax.rem(team + ahead, teams)
+        return pltpu.make_async_remote_copy(
+            src_ref=cur.at[pl.ds(goal * few, few)], dst_ref=arrived.at[team],
+            send_sem=gather_send.at[5, ahead], recv_sem=gather_recv.at[5, ahead],
+            device_id=at(ahead), device_id_type=MESH,
+        )
+
+    for ahead in others:
+        deliver(ahead).start()
+    for p in range(few):
+        arrived[team, p] = cur[team * few + p]
+    for ahead in others:
+        deliver(ahead).wait()
+    for p in range(few):
+        for c in range(0, teams, 2):
+            one, two = arrived[c, p], arrived[c + 1, p]
+            out[2 * p, c * width : c * width + 8, :] = jnp.where(half, one, pltpu.roll(two, width, 0))
+            out[2 * p + 1, c * width : c * width + 8, :] = jnp.where(half, pltpu.roll(one, width, 0), two)
+
+
+def bed(teams, probe, positions, conductivity, fluid_exchange, row_blocks, column_blocks):
+    rows, columns, particles = probe.shape
+    slots = column_blocks.shape[1]
+    clusters = teams * rows
+    total = MEAN_BLOCKS * clusters
+    units = total // 4
+    span = 2 * units
+    pairs = clusters // 2
+    f32, bf16, i32 = jnp.float32, jnp.bfloat16, jnp.int32
+    vmem = pl.BlockSpec(memory_space=pltpu.VMEM)
+    anywhere = pl.BlockSpec(memory_space=pl.ANY)
+    field = pltpu.VMEM((pairs, 8, particles), f32)
+    return pl.pallas_call(
+        functools.partial(bed_kernel, teams, total),
+        out_shape=jax.ShapeDtypeStruct((rows, columns, particles), f32),
+        in_specs=[anywhere] * 6,
+        out_specs=vmem,
+        scratch_shapes=[
+            pltpu.VMEM(probe.shape, probe.dtype),
+            pltpu.VMEM(positions.shape, f32),
+            pltpu.VMEM(conductivity.shape, f32),
+            pltpu.SemaphoreType.DMA((6,)),
+            pltpu.VMEM((teams, rows, 4, particles), f32),
+            pltpu.VMEM((teams, rows, slots), i32),
+            pltpu.VMEM((teams, 1, rows), i32),
+            pltpu.SMEM((teams, 1, rows), i32),
+            pltpu.SMEM((clusters, slots), i32),
+            pltpu.SemaphoreType.DMA((teams + 1,)),
+            pltpu.VMEM((teams, rows, particles), f32),
+            pltpu.VMEM((teams, rows // 4, 16, particles), bf16),
+            pltpu.VMEM((teams, rows // 4, 16, particles), bf16),
+            pltpu.VMEM((clusters, 4, particles, particles), f32),
+            pltpu.VMEM((units, 2 * particles, particles), bf16),
+            pltpu.SMEM((clusters + 1,), i32),
+            pltpu.SMEM((clusters + 1,), i32),
+            pltpu.SMEM((span,), i32),
+            pltpu.SMEM((span,), f32),
+            pltpu.SMEM((span,), f32),
+            pltpu.SMEM((slots,), f32),
+            pltpu.SMEM((clusters,), i32),
+            pltpu.VMEM((span + 1, 8, particles), f32),
+            pltpu.VMEM((span + 1, 8, particles), f32),
+            pltpu.VMEM((clusters, 16, particles), bf16),
+            pltpu.VMEM((clusters, 16, particles), bf16),
+            field, field, field, field,
+            pltpu.VMEM((2, pairs, 8, particles), f32),
+            pltpu.VMEM((2, pairs, 8, particles), f32),
+            field, field,
+            pltpu.VMEM((teams, rows // 2, 8, particles), f32),
+            pltpu.SemaphoreType.DMA((6, teams)),
+            pltpu.SemaphoreType.DMA((6, teams)),
+            pltpu.SemaphoreType.DMA((3,)),
+            pltpu.SemaphoreType.DMA((3,)),
+        ],
+        compiler_params=pltpu.CompilerParams(
+            collective_id=1, has_side_effects=True, vmem_limit_bytes=60 * 1024 * 1024
+        ),
+    )(probe, positions, conductivity, fluid_exchange, row_blocks.reshape(1, rows), column_blocks)
+
+
+def either(teams, probe, *rest):
+    rows, columns, particles = probe.shape
+    if columns == 4 * teams and rows % 4 == 0 and MEAN_BLOCKS * teams * rows <= 1024:
+        return bed(teams, probe, *rest)
+    return local(teams, probe, *rest)
+
+
 def solution(mesh):
     return jax.shard_map(
-        functools.partial(local, mesh.shape["blk"]),
+        functools.partial(either, mesh.shape["blk"]),
         mesh=mesh,
         in_specs=(
             P(("groups", "blk"), None, None),

time: 77.8 us -> 77.1 us (level)
  Pallas kernels: 76.1 us -> 75.3 us
where the time goes in v1:
time: 77.1 us; the launch traced here: 77 us
  Pallas kernels  75.3 us (98%)
  local copies, waits for them, and re-layouts  1.62 us (2%)
    pallas_call x1, Pallas kernels, bed(): pl.pallas_call(functools.partial(bed_kernel, teams, total), out_shape=jax...  75.3 us
    unnamed x1, local copies, waits for them, and re-layouts  1.62 us

profile of v1, /device:TPU:0, one launch (start us, length us, event | category | flops | bytes accessed | tf_op | source)
XLA Modules:
  0.0 77.0 jit_solution(608276504796179327)
XLA Ops:
  0.0 75.3 %shard_map.64 = f32[12,32,128]{2,1,0:T(8,128)} custom-call(bf16[12,32,128]{2,1,0:T(8,128)(2,1)} %probe_in.1, f32[12,3,128]{2,1,0:T(4,128)} %pos_in.1, f32[12,128]{1,0:T(8,128)} %cond_in.1, f32[12,128]{1,0:T(8,128)} %fluid_in.1, s32[1,12]{1,0:T(1,128)} %bitcast.1, s32[12,27]{1,0:T(8,128)} %cols_in.1), custom_call_target="tpu_custom_call" | custom-call | tf_op jit(solution)/shard_map/pallas_call | solution.py:560
  75.4 1.6 %copy.8 = f32[12,32,128]{2,1,0:T(8,128)} copy(f32[12,32,128]{2,1,0:T(8,128)} %shard_map.64) | data formatting | bytes 393216

commit v2 on v1

--- a/solution.py
+++ b/solution.py
@@ -18,7 +18,9 @@
 CHUNK = 3
 MEAN_BLOCKS = 9
 APPROX = True
-UNROLL = 54
+UNROLL = 216
+BUILD = 24
+SPREAD = 12
 
 
 def kernel(
@@ -247,7 +249,7 @@
     teams, total, probe_in, pos_in, cond_in, fluid_in, counts_in, cols_in, out,
     probe, pos, cond, load_sem,
     geo, ints, cnts, counts, cols, smem_sem, fluid, stage, landed,
-    bcast, tiles, ends, begins, ids, keep, selfs, more, last,
+    points, mid, lines, flank, tiles, ends, begins, ids, keep, selfs, more, last,
     sums, parts, low, high, cur, prev, inv, corr, mine_sum, their_sum, mine_deg, their_deg, arrived,
     gather_send, gather_recv, pair_send, pair_recv,
 ):
@@ -310,13 +312,60 @@
         gather(0, ahead).start()
         gather(1, ahead).start()
 
+    level = lax.broadcasted_iota(jnp.int32, (8, particles), 0)
+    half = level < width
+    square = level % width == 3
+
+    def rounded(value):
+        return value.astype(bf16).astype(f32)
+
+    def thirds(value):
+        head = rounded(value)
+        tail = value - head
+        body = rounded(tail)
+        return head, body, tail - body
+
+    def length(value):
+        value = value * value
+        value = value + pltpu.roll(value, 1, 0)
+        return value + pltpu.roll(value, 2, 0)
+
     def spread(place):
         def one(r, carry):
-            for k in range(4):
-                line = geo[place, r, k : k + 1, :]
-                bcast[place * rows + r, k] = jnp.broadcast_to(line, (particles, particles)).T
+            spot = place * rows + r
+            point = geo[place, r]
+            point = jnp.where(square, 0.0, jnp.concatenate([point, point], 0))
+            middle = jnp.broadcast_to(jnp.sum(point * (1.0 / particles), axis=1, keepdims=True), (8, particles))
+            points[spot] = point
+            mid[spot] = middle
+            off = point - middle
+            a, b, c = thirds(off)
+            d, e, f = thirds(length(off))
+            g, h, i = thirds(jnp.broadcast_to(geo[place, r, 3:4, :], (8, particles)))
+            last_line = jnp.zeros((8, particles), f32)
+            for n, value in enumerate((d, e, f, g, h, i)):
+                last_line = jnp.where(level == n, value, last_line)
+            block = jnp.concatenate(
+                [
+                    jnp.where(level == 3, 1.0, jnp.where(half, a, b)),
+                    jnp.where(level == 7, 1.0, jnp.where(half, c, a)),
+                    jnp.where(level == 7, 1.0, jnp.where(half, b, a)),
+                    last_line,
+                ],
+                0,
+            )
+            lines[spot] = block.T.astype(bf16)
+            flank[spot] = jnp.concatenate(
+                [
+                    jnp.where(level == 3, g, 0.0),
+                    jnp.where(level == 7, h, 0.0),
+                    jnp.where(level == 7, i, 0.0),
+                    jnp.where((level > 2) & (level < 6), 1.0, 0.0),
+                ],
+                0,
+            ).astype(bf16)
             return carry
-        lax.fori_loop(0, rows, one, 0, unroll=4)
+        lax.fori_loop(0, rows, one, 0, unroll=SPREAD)
 
     spread(team)
     loads[2].wait()
@@ -361,6 +410,8 @@
 
     _, zero, one = lax.fori_loop(0, teams, lay, (jnp.int32(0), jnp.int32(0), jnp.int32(0)))
     zero, one = jnp.minimum(zero, clusters - 1), jnp.minimum(one, clusters - 1)
+
+    ones = jnp.where(level < 3, 1.0, 0.0)
 
     def build_tile(u, lane, r, selves, running):
         place = first + lane * units + u
@@ -374,17 +425,18 @@
         keep[index] = going
         selves = jnp.where(fresh, 0.0, selves) + jnp.where(col == r, 1.0, 0.0)
         selfs[index] = selves
-        t = lax.div(r, rows)
-        xi = [jnp.broadcast_to(geo[t, r - t * rows, k : k + 1, :], (8, particles)) for k in range(4)]
+        off = points[r] - mid[col]
+        a, b, c = thirds(jnp.where(square, length(off), -2.0 * off))
+        block = jnp.concatenate([a, jnp.where(half, a, b), jnp.where(half, b, c), ones], 0).astype(bf16)
+        both_sides = jnp.dot(
+            lines[col], jnp.concatenate([block, flank[r]], 1), preferred_element_type=f32
+        )
         tally = jnp.zeros((8, particles), f32)
         for j in range(0, particles, 16):
             values = []
             for h in (j, j + 8):
-                dx = bcast[col, 0, h : h + 8, :] - xi[0]
-                dy = bcast[col, 1, h : h + 8, :] - xi[1]
-                dz = bcast[col, 2, h : h + 8, :] - xi[2]
-                power = dx * dx + dy * dy + dz * dz
-                value = pltpu.reciprocal((bcast[col, 3, h : h + 8, :] + xi[3]) * jnp.exp2(power), approx=APPROX)
+                power = both_sides[h : h + 8, :particles]
+                value = pltpu.reciprocal(both_sides[h : h + 8, particles:] * jnp.exp2(power), approx=APPROX)
                 tally = tally + value
                 values.append(value)
             tiles[u, lane * particles + j : lane * particles + j + 16, :] = jnp.concatenate(values, 0).astype(bf16)
@@ -397,7 +449,7 @@
 
     blank = jnp.zeros((8, particles), f32)
     state = lax.fori_loop(
-        0, units, build, (zero, jnp.float32(0.0), blank, one, jnp.float32(0.0), blank), unroll=2
+        0, units, build, (zero, jnp.float32(0.0), blank, one, jnp.float32(0.0), blank), unroll=BUILD
     )
 
     sums[span] = blank
@@ -409,8 +461,6 @@
         more[u] = flag
         selfs[units + u] = selfs[units + u] + flag * selfs[units - 1]
         sums[units + u] = sums[units + u] + flag * sums[units - 1]
-    half = lax.broadcasted_iota(jnp.int32, (8, particles), 0) < width
-
     def both(even, odd):
         return jnp.where(half, jnp.broadcast_to(even, (8, particles)), jnp.broadcast_to(odd, (8, particles)))
 
@@ -468,17 +518,6 @@
 
     lax.fori_loop(0, teams, begin_fields, 0)
 
-    degrees.wait()
-
-    def divide(t, carry):
-        for j in range(0, rows, 2):
-            p = t * (rows // 2) + j // 2
-            exchange = both(fluid[t, j : j + 1, :], fluid[t, j + 1 : j + 2, :])
-            inv[p] = (2.0 / HALF_SPAN) / (exchange + (mine_deg[p] + their_deg[p]))
-        return carry
-
-    lax.fori_loop(0, teams, divide, 0)
-
     def step(k, carry):
         slot = lax.rem(k, 2)
 
@@ -504,6 +543,20 @@
         lax.fori_loop(0, pairs, pack, 0, unroll=8)
         exchange = swap(mine_sum.at[slot], their_sum.at[slot], slot)
         exchange.start()
+
+        @pl.when(k == 0)
+        def _():
+            degrees.wait()
+
+            def divide(t, carry):
+                for j in range(0, rows, 2):
+                    p = t * (rows // 2) + j // 2
+                    exchange = both(fluid[t, j : j + 1, :], fluid[t, j + 1 : j + 2, :])
+                    inv[p] = (2.0 / HALF_SPAN) / (exchange + (mine_deg[p] + their_deg[p]))
+                return carry
+
+            lax.fori_loop(0, teams, divide, 0)
+
         exchange.wait()
         gain = jnp.where(k == 0, 0.5, 1.0)
 
@@ -576,7 +629,10 @@
             pltpu.VMEM((teams, rows, particles), f32),
             pltpu.VMEM((teams, rows // 4, 16, particles), bf16),
             pltpu.VMEM((teams, rows // 4, 16, particles), bf16),
-            pltpu.VMEM((clusters, 4, particles, particles), f32),
+            pltpu.VMEM((clusters, 8, particles), f32),
+            pltpu.VMEM((clusters, 8, particles), f32),
+            pltpu.VMEM((clusters, particles, 32), bf16),
+            pltpu.VMEM((clusters, 32, particles), bf16),
             pltpu.VMEM((units, 2 * particles, particles), bf16),
             pltpu.SMEM((clusters + 1,), i32),
             pltpu.SMEM((clusters + 1,), i32),

time: 77.1 us -> 63.3 us (0.82)
  Pallas kernels: 75.3 us -> 61.6 us
    pallas_call x1, Pallas kernels: 75.3 us -> 61.6 us  [bed(): pl.pallas_call(functools.partial(bed_kernel, teams, total), out_shape=jax...]
where the time goes in v2:
time: 63.3 us; the launch traced here: 63.2 us
  Pallas kernels  61.6 us (97%)
  local copies, waits for them, and re-layouts  1.62 us (3%)
    pallas_call x1, Pallas kernels, bed(): pl.pallas_call(functools.partial(bed_kernel, teams, total), out_shape=jax...  61.6 us
    unnamed x1, local copies, waits for them, and re-layouts  1.62 us

profile of v2, /device:TPU:0, one launch (start us, length us, event | category | flops | bytes accessed | tf_op | source)
XLA Modules:
  0.0 63.2 jit_solution(3730546707901553712)
XLA Ops:
  0.0 61.6 %shard_map.64 = f32[12,32,128]{2,1,0:T(8,128)} custom-call(bf16[12,32,128]{2,1,0:T(8,128)(2,1)} %probe_in.1, f32[12,3,128]{2,1,0:T(4,128)} %pos_in.1, f32[12,128]{1,0:T(8,128)} %cond_in.1, f32[12,128]{1,0:T(8,128)} %fluid_in.1, s32[1,12]{1,0:T(1,128)} %bitcast.1, s32[12,27]{1,0:T(8,128)} %cols_in.1), custom_call_target="tpu_custom_call" | custom-call | tf_op jit(solution)/shard_map/pallas_call | solution.py:613
  61.6 1.6 %copy.8 = f32[12,32,128]{2,1,0:T(8,128)} copy(f32[12,32,128]{2,1,0:T(8,128)} %shard_map.64) | data formatting | bytes 393216

commit v3 on v2

--- a/solution.py
+++ b/solution.py
@@ -20,6 +20,7 @@
 APPROX = True
 UNROLL = 216
 BUILD = 24
+PIECES = 2
 SPREAD = 12
 
 
@@ -279,7 +280,7 @@
         for n, (source, place) in enumerate(
             (
                 (pos_in, pos), (cond_in, cond), (probe_in, probe),
-                (cols_in, ints.at[team]), (counts_in, cnts.at[team]), (fluid_in, fluid.at[team]),
+                (cols_in, cols.at[pl.ds(team * rows, rows)]), (counts_in, counts.at[team]), (fluid_in, fluid.at[team]),
             )
         )
     ]
@@ -294,7 +295,7 @@
 
     def gather(kind, ahead):
         source, place = (
-            (counts_in, cnts.at[team]), (cols_in, ints.at[team]), (geo.at[team], geo.at[team]),
+            (counts.at[team], counts.at[team]), (cols.at[pl.ds(team * rows, rows)], cols.at[pl.ds(team * rows, rows)]), (geo.at[team], geo.at[team]),
             (stage.at[lax.rem(team + ahead, teams)], landed.at[team]), (fluid_in, fluid.at[team]),
         )[kind]
         return pltpu.make_async_remote_copy(
@@ -307,10 +308,10 @@
     for load in loads[3:5]:
         load.wait()
     for ahead in others:
-        gather(2, ahead).start()
-    for ahead in others:
         gather(0, ahead).start()
         gather(1, ahead).start()
+    for ahead in others:
+        gather(2, ahead).start()
 
     level = lax.broadcasted_iota(jnp.int32, (8, particles), 0)
     half = level < width
@@ -354,7 +355,7 @@
                 ],
                 0,
             )
-            lines[spot] = block.T.astype(bf16)
+            lines[spot] = block.astype(bf16).T
             flank[spot] = jnp.concatenate(
                 [
                     jnp.where(level == 3, g, 0.0),
@@ -378,22 +379,6 @@
     for ahead in others:
         gather(0, ahead).wait()
         gather(1, ahead).wait()
-    moves = [
-        pltpu.make_async_copy(cnts, counts, smem_sem.at[teams]),
-    ] + [
-        pltpu.make_async_copy(ints.at[t], cols.at[pl.ds(t * rows, rows)], smem_sem.at[t]) for t in range(teams)
-    ]
-    for move in moves:
-        move.start()
-    for ahead in others:
-        gather(2, ahead).wait()
-        spread(lax.rem(team + teams - ahead, teams))
-    for ahead in others:
-        gather(3, ahead).start()
-        gather(4, ahead).start()
-    for move in moves:
-        move.wait()
-
     first = member * span
     final = first + span
 
@@ -410,6 +395,14 @@
 
     _, zero, one = lax.fori_loop(0, teams, lay, (jnp.int32(0), jnp.int32(0), jnp.int32(0)))
     zero, one = jnp.minimum(zero, clusters - 1), jnp.minimum(one, clusters - 1)
+
+    for ahead in others:
+        gather(2, ahead).wait()
+        spread(lax.rem(team + teams - ahead, teams))
+    for ahead in others:
+        gather(3, ahead).start()
+        gather(4, ahead).start()
+
 
     ones = jnp.where(level < 3, 1.0, 0.0)
 
@@ -540,9 +533,17 @@
             mine_sum[slot, p] = product - corr[p] * own
             return carry
 
-        lax.fori_loop(0, pairs, pack, 0, unroll=8)
-        exchange = swap(mine_sum.at[slot], their_sum.at[slot], slot)
-        exchange.start()
+        share = pairs // PIECES
+        exchanges = [
+            swap(
+                mine_sum.at[slot, pl.ds(n * share, share)], their_sum.at[slot, pl.ds(n * share, share)],
+                3 + 2 * n + slot,
+            )
+            for n in range(PIECES)
+        ]
+        for n in range(PIECES):
+            lax.fori_loop(n * share, (n + 1) * share, pack, 0, unroll=8)
+            exchanges[n].start()
 
         @pl.when(k == 0)
         def _():
@@ -557,7 +558,6 @@
 
             lax.fori_loop(0, teams, divide, 0)
 
-        exchange.wait()
         gain = jnp.where(k == 0, 0.5, 1.0)
 
         def update(p, carry):
@@ -570,7 +570,9 @@
             publish(p, fresh)
             return carry
 
-        lax.fori_loop(0, pairs, update, 0, unroll=8)
+        for n in range(PIECES):
+            exchanges[n].wait()
+            lax.fori_loop(n * share, (n + 1) * share, update, 0, unroll=8)
         return carry
 
     lax.fori_loop(0, DEGREE, step, 0)
@@ -652,8 +654,8 @@
             pltpu.VMEM((teams, rows // 2, 8, particles), f32),
             pltpu.SemaphoreType.DMA((6, teams)),
             pltpu.SemaphoreType.DMA((6, teams)),
-            pltpu.SemaphoreType.DMA((3,)),
-            pltpu.SemaphoreType.DMA((3,)),
+            pltpu.SemaphoreType.DMA((3 + 2 * PIECES,)),
+            pltpu.SemaphoreType.DMA((3 + 2 * PIECES,)),
         ],
         compiler_params=pltpu.CompilerParams(
             collective_id=1, has_side_effects=True, vmem_limit_bytes=60 * 1024 * 1024

time: 63.3 us -> 58.8 us (0.929)
  Pallas kernels: 61.6 us -> 57 us
    pallas_call x1, Pallas kernels: 61.6 us -> 57 us  [bed(): pl.pallas_call(functools.partial(bed_kernel, teams, total), out_shape=jax...]
where the time goes in v3:
time: 58.8 us; the launch traced here: 58.6 us
  Pallas kernels  57 us (97%)
  local copies, waits for them, and re-layouts  1.62 us (3%)
    pallas_call x1, Pallas kernels, bed(): pl.pallas_call(functools.partial(bed_kernel, teams, total), out_shape=jax...  57 us
    unnamed x1, local copies, waits for them, and re-layouts  1.62 us

profile of v3, /device:TPU:0, one launch (start us, length us, event | category | flops | bytes accessed | tf_op | source)
XLA Modules:
  0.0 58.6 jit_solution(7699887831975374513)
XLA Ops:
  0.0 57.0 %shard_map.64 = f32[12,32,128]{2,1,0:T(8,128)} custom-call(bf16[12,32,128]{2,1,0:T(8,128)(2,1)} %probe_in.1, f32[12,3,128]{2,1,0:T(4,128)} %pos_in.1, f32[12,128]{1,0:T(8,128)} %cond_in.1, f32[12,128]{1,0:T(8,128)} %fluid_in.1, s32[1,12]{1,0:T(1,128)} %bitcast.1, s32[12,27]{1,0:T(8,128)} %cols_in.1), custom_call_target="tpu_custom_call" | custom-call | tf_op jit(solution)/shard_map/pallas_call | solution.py:615
  57.0 1.6 %copy.8 = f32[12,32,128]{2,1,0:T(8,128)} copy(f32[12,32,128]{2,1,0:T(8,128)} %shard_map.64) | data formatting | bytes 393216

commit v4 on v3

--- a/solution.py
+++ b/solution.py
@@ -19,7 +19,7 @@
 MEAN_BLOCKS = 9
 APPROX = True
 UNROLL = 216
-BUILD = 24
+BUILD = 54
 PIECES = 2
 SPREAD = 12
 
@@ -305,12 +305,13 @@
         )
 
     others = range(1, teams)
+    order = sorted(others, key=lambda a: -abs(2 * a - teams))
     for load in loads[3:5]:
         load.wait()
     for ahead in others:
         gather(0, ahead).start()
         gather(1, ahead).start()
-    for ahead in others:
+    for ahead in order:
         gather(2, ahead).start()
 
     level = lax.broadcasted_iota(jnp.int32, (8, particles), 0)
@@ -396,7 +397,7 @@
     _, zero, one = lax.fori_loop(0, teams, lay, (jnp.int32(0), jnp.int32(0), jnp.int32(0)))
     zero, one = jnp.minimum(zero, clusters - 1), jnp.minimum(one, clusters - 1)
 
-    for ahead in others:
+    for ahead in order:
         gather(2, ahead).wait()
         spread(lax.rem(team + teams - ahead, teams))
     for ahead in others:

time: 58.8 us -> 57.5 us (0.978)
  Pallas kernels: 57 us -> 55.7 us
    pallas_call x1, Pallas kernels: 57 us -> 55.7 us  [bed(): pl.pallas_call(functools.partial(bed_kernel, teams, total), out_shape=jax...]
where the time goes in v4:
time: 57.5 us; the launch traced here: 57.3 us
  Pallas kernels  55.7 us (97%)
  local copies, waits for them, and re-layouts  1.62 us (3%)
    pallas_call x1, Pallas kernels, bed(): pl.pallas_call(functools.partial(bed_kernel, teams, total), out_shape=jax...  55.7 us
    unnamed x1, local copies, waits for them, and re-layouts  1.62 us

profile of v4, /device:TPU:0, one launch (start us, length us, event | category | flops | bytes accessed | tf_op | source)
XLA Modules:
  0.0 57.3 jit_solution(15463364261734337807)
XLA Ops:
  0.0 55.7 %shard_map.64 = f32[12,32,128]{2,1,0:T(8,128)} custom-call(bf16[12,32,128]{2,1,0:T(8,128)(2,1)} %probe_in.1, f32[12,3,128]{2,1,0:T(4,128)} %pos_in.1, f32[12,128]{1,0:T(8,128)} %cond_in.1, f32[12,128]{1,0:T(8,128)} %fluid_in.1, s32[1,12]{1,0:T(1,128)} %bitcast.1, s32[12,27]{1,0:T(8,128)} %cols_in.1), custom_call_target="tpu_custom_call" | custom-call | tf_op jit(solution)/shard_map/pallas_call | solution.py:616
  55.7 1.6 %copy.8 = f32[12,32,128]{2,1,0:T(8,128)} copy(f32[12,32,128]{2,1,0:T(8,128)} %shard_map.64) | data formatting | bytes 393216

commit v5 on v4

--- a/solution.py
+++ b/solution.py
@@ -20,7 +20,7 @@
 APPROX = True
 UNROLL = 216
 BUILD = 54
-PIECES = 2
+PIECES = 3
 SPREAD = 12
 
 
@@ -477,7 +477,7 @@
             corr[p] = both(lines[0][1], lines[1][1])
         return carry
 
-    lax.fori_loop(0, teams, settle, 0)
+    lax.fori_loop(0, teams, settle, 0, unroll=4)
 
     def swap(source, place, n):
         return pltpu.make_async_remote_copy(
@@ -510,7 +510,7 @@
                 publish(p, block[8 * h : 8 * h + 8])
         return carry
 
-    lax.fori_loop(0, teams, begin_fields, 0)
+    lax.fori_loop(0, teams, begin_fields, 0, unroll=2)
 
     def step(k, carry):
         slot = lax.rem(k, 2)
@@ -557,7 +557,7 @@
                     inv[p] = (2.0 / HALF_SPAN) / (exchange + (mine_deg[p] + their_deg[p]))
                 return carry
 
-            lax.fori_loop(0, teams, divide, 0)
+            lax.fori_loop(0, teams, divide, 0, unroll=2)
 
         gain = jnp.where(k == 0, 0.5, 1.0)
 

time: 57.5 us -> 57.1 us (level)
  no operation moved by 1% of the time
where the time goes in v5:
time: 57.1 us; the launch traced here: 56.9 us
  Pallas kernels  55.3 us (97%)
  local copies, waits for them, and re-layouts  1.62 us (3%)
    pallas_call x1, Pallas kernels, bed(): pl.pallas_call(functools.partial(bed_kernel, teams, total), out_shape=jax...  55.3 us
    unnamed x1, local copies, waits for them, and re-layouts  1.62 us

profile of v5, /device:TPU:0, one launch (start us, length us, event | category | flops | bytes accessed | tf_op | source)
XLA Modules:
  0.0 56.9 jit_solution(6300222449340017407)
XLA Ops:
  0.0 55.3 %shard_map.64 = f32[12,32,128]{2,1,0:T(8,128)} custom-call(bf16[12,32,128]{2,1,0:T(8,128)(2,1)} %probe_in.1, f32[12,3,128]{2,1,0:T(4,128)} %pos_in.1, f32[12,128]{1,0:T(8,128)} %cond_in.1, f32[12,128]{1,0:T(8,128)} %fluid_in.1, s32[1,12]{1,0:T(1,128)} %bitcast.1, s32[12,27]{1,0:T(8,128)} %cols_in.1), custom_call_target="tpu_custom_call" | custom-call | tf_op jit(solution)/shard_map/pallas_call | solution.py:616
  55.3 1.6 %copy.8 = f32[12,32,128]{2,1,0:T(8,128)} copy(f32[12,32,128]{2,1,0:T(8,128)} %shard_map.64) | data formatting | bytes 393216

commit v6 on v5

--- a/solution.py
+++ b/solution.py
@@ -477,7 +477,7 @@
             corr[p] = both(lines[0][1], lines[1][1])
         return carry
 
-    lax.fori_loop(0, teams, settle, 0, unroll=4)
+    lax.fori_loop(0, teams, settle, 0, unroll=8)
 
     def swap(source, place, n):
         return pltpu.make_async_remote_copy(
@@ -510,7 +510,7 @@
                 publish(p, block[8 * h : 8 * h + 8])
         return carry
 
-    lax.fori_loop(0, teams, begin_fields, 0, unroll=2)
+    lax.fori_loop(0, teams, begin_fields, 0, unroll=4)
 
     def step(k, carry):
         slot = lax.rem(k, 2)

time: 57.1 us -> 57 us (level)
  no operation moved by 1% of the time
where the time goes in v6:
time: 57 us; the launch traced here: 56.9 us
  Pallas kernels  55.2 us (97%)
  local copies, waits for them, and re-layouts  1.62 us (3%)
    pallas_call x1, Pallas kernels, bed(): pl.pallas_call(functools.partial(bed_kernel, teams, total), out_shape=jax...  55.2 us
    unnamed x1, local copies, waits for them, and re-layouts  1.62 us

profile of v6, /device:TPU:0, one launch (start us, length us, event | category | flops | bytes accessed | tf_op | source)
XLA Modules:
  0.0 56.9 jit_solution(14494955205178308593)
XLA Ops:
  0.0 55.2 %shard_map.64 = f32[12,32,128]{2,1,0:T(8,128)} custom-call(bf16[12,32,128]{2,1,0:T(8,128)(2,1)} %probe_in.1, f32[12,3,128]{2,1,0:T(4,128)} %pos_in.1, f32[12,128]{1,0:T(8,128)} %cond_in.1, f32[12,128]{1,0:T(8,128)} %fluid_in.1, s32[1,12]{1,0:T(1,128)} %bitcast.1, s32[12,27]{1,0:T(8,128)} %cols_in.1), custom_call_target="tpu_custom_call" | custom-call | tf_op jit(solution)/shard_map/pallas_call | solution.py:616
  55.2 1.6 %copy.8 = f32[12,32,128]{2,1,0:T(8,128)} copy(f32[12,32,128]{2,1,0:T(8,128)} %shard_map.64) | data formatting | bytes 393216
